TPU v7x, 32 devices: a whole 2x2x4 slice. The times are simulated.
32 devices in a mesh: group: 4 (over x, core), expert: 8 (over z, y).
Axes of the slice: x: 2, y: 2, z: 4, core: 2. Of those that a mesh axis runs over, the one named last changes fastest.
Arguments:
- out_grad: bfloat16 [8192, 3584], P(('group', 'expert')), may hold values from -6 to 6
- gates: float32 [8192, 8], P(('group', 'expert')), may hold values from 0.05 to 0.6
- routes: int32 [8192, 8], P(('group', 'expert')), may hold values from 0 to 23, all different within a row
- copy_pick: int32 [8192, 8], P(('group', 'expert')), may hold values from 0 to 839
- replica_plan: int32 [8], replicated, may hold values from 0 to 5, as said below
- down_weight: bfloat16 [8, 1024, 3584], P('expert'), as said below
- saved_hidden: bfloat16 [4, 8, 8, 80, 1024], P('group', 'expert'), may hold values from -0.75 to 0.75
Outputs:
- route_grad: float32 [8192, 8], P(('group', 'expert'))
- hidden_grad: bfloat16 [4, 8, 8, 80, 1024], P('group', 'expert')
- copy_grad: bfloat16 [8, 1024, 3584], P('expert', 'group')
Inputs may be any that keep to these rules, and one draw needn't show every extreme that they name: `replica_plan`: every expert 0 to 5 is served by at least one slot; exactly 2 experts are served by more than one slot. `down_weight`: slots that serve the same expert hold equal weights.
All inputs are finite; a program needn't handle non-finite values.
Results may differ from a plain program's by a relative error of at most 0.019.
Values may be sent and summed in bfloat16 or wider, within the bound.
No kernel may reach another device: no remote copies, remote signals or barrier semaphores. Data moves between devices by JAX's collectives and lax.ppermute only.
A program may use at most 128 MiB of HBM per device.

v0:
```python
import functools
import itertools

import jax
import jax.numpy as jnp
import numpy as np
from jax import lax
from jax.experimental import pallas as pl
from jax.experimental.pallas import tpu as pltpu
from jax.sharding import PartitionSpec as P

HOT = 2
tile = 512


def tile_of(width, start=0):
    return next(t for t in (512, 896, 640, 384, 256, 128, width) if width % t == 0 and start % t == 0)


def cost(flops):
    return pl.CostEstimate(flops=flops, bytes_accessed=flops // 300, transcendentals=0)
CHUNKS = (2048, 1024, 512)


def slot_layout(replica_plan):
    slot_count = replica_plan.shape[0]
    slot_ids = jnp.arange(slot_count, dtype=jnp.int32)
    same_expert = replica_plan[:, None] == replica_plan[None, :]
    earlier_slot = slot_ids[None, :] < slot_ids[:, None]
    ordinal = jnp.sum(same_expert & earlier_slot, axis=1)
    return (slot_ids, same_expert, ordinal)


def route_kernel(
    expert_count, cap_rows, seat, slot_plan, plan_row, routes, picks, gates, spread, rank_out, slot_out
):
    slot_count = plan_row.shape[1]
    top_count, tokens = routes.shape
    column = lax.broadcasted_iota(jnp.int32, (slot_count, 1), 0)
    plan = jnp.zeros((slot_count, 1), jnp.int32)
    for s in range(slot_count):
        plan = jnp.where(column == s, slot_plan[s], plan)
    same = plan == plan_row[...]
    slot_r = lax.broadcasted_iota(jnp.int32, (slot_count, slot_count), 0)
    slot_c = lax.broadcasted_iota(jnp.int32, (slot_count, slot_count), 1)
    copies = jnp.sum(jnp.where(same, 1.0, 0.0), axis=1, keepdims=True)
    ordinal = jnp.sum(jnp.where(same & (slot_c < slot_r), 1.0, 0.0), axis=1, keepdims=True)
    slot_ids = lax.broadcasted_iota(jnp.int32, (slot_count, tokens), 0)
    reach = jnp.zeros((slot_count, tokens), jnp.float32)
    gate_of = jnp.zeros((slot_count, tokens), jnp.float32)
    matches = []
    for k in range(top_count):
        route = routes[k : k + 1, :]
        pick = picks[k : k + 1, :].astype(jnp.float32)
        chosen = pick - copies * jnp.floor((pick + 0.5) / copies)
        match = (route == plan) & (chosen == ordinal) & (route < expert_count)
        matches.append(match)
        reach = jnp.where(match, 1.0, reach)
        gate_of = jnp.where(match, gates[k : k + 1, :], gate_of)
    before = lax.broadcasted_iota(jnp.int32, (tokens, tokens), 0) < lax.broadcasted_iota(
        jnp.int32, (tokens, tokens), 1
    )
    rank = lax.dot_general(
        reach.astype(jnp.bfloat16),
        jnp.where(before, 1.0, 0.0).astype(jnp.bfloat16),
        (((1,), (0,)), ((), ())),
        preferred_element_type=jnp.float32,
    ).astype(jnp.int32)
    kept = (reach > 0.0) & (rank < cap_rows)
    rank = jnp.where(kept, rank, -1)
    rank_out[...] = rank
    for k in range(top_count):
        slot_out[k : k + 1, :] = (
            jnp.sum(jnp.where(matches[k] & kept, slot_ids + 1, 0), axis=0, keepdims=True) - 1
        )
    row_ids = lax.broadcasted_iota(jnp.int32, spread.shape[1:], 0)
    for s in range(slot_count):
        placed = jnp.where(row_ids == rank[s : s + 1, :], gate_of[s : s + 1, :], 0.0)
        spread[seat[0] ^ s] = placed.astype(jnp.bfloat16)


def place_routes(routes, picks, gates, replica_plan, seat, expert_count, cap_rows, held_rows):
    slot_count = replica_plan.shape[0]
    top_count, tokens = routes.shape
    vmem = pl.BlockSpec(memory_space=pltpu.VMEM)
    return pl.pallas_call(
        functools.partial(route_kernel, expert_count, cap_rows),
        out_shape=(
            jax.ShapeDtypeStruct((slot_count, held_rows, tokens), jnp.bfloat16),
            jax.ShapeDtypeStruct((slot_count, tokens), jnp.int32),
            jax.ShapeDtypeStruct((top_count, tokens), jnp.int32),
        ),
        in_specs=[pl.BlockSpec(memory_space=pltpu.SMEM)] * 2 + [vmem] * 4,
        out_specs=(vmem, vmem, vmem),
    )(seat, replica_plan, replica_plan.reshape(1, slot_count), routes, picks, gates)


def send_all_kernel(seat, spread, rows, *rest):
    out = rest[-1]
    held_rows, tokens = spread.shape[1:]
    total = jnp.dot(spread[...].reshape(-1, tokens), rows[...], preferred_element_type=jnp.float32)
    for d in range(spread.shape[0]):
        out[seat[0] ^ d] = total[d * held_rows : (d + 1) * held_rows].astype(jnp.bfloat16)


def all_rows_to_send(spread, out_grad, seat, span, after):
    slot_count, held_rows, tokens = spread.shape
    start, stop = span
    tile = tile_of(stop - start, start)
    return pl.pallas_call(
        send_all_kernel,
        grid=((stop - start) // tile,),
        in_specs=[
            pl.BlockSpec(memory_space=pltpu.SMEM),
            pl.BlockSpec((slot_count, held_rows, tokens), lambda j: (0, 0, 0)),
            pl.BlockSpec((tokens, tile), lambda j: (0, start // tile + j)),
        ]
        + [pl.BlockSpec(memory_space=pl.ANY)] * len(after),
        out_specs=pl.BlockSpec((slot_count, held_rows, tile), lambda j: (0, 0, j)),
        out_shape=jax.ShapeDtypeStruct((slot_count, held_rows, stop - start), jnp.bfloat16),
        cost_estimate=cost(2 * slot_count * held_rows * tokens * (stop - start)),
    )(seat, spread, out_grad, *after)


def part_kernel(leave, rows, *rest):
    flat = rows[...].reshape(-1, rows.shape[-1])
    rest[-1][...] = jnp.dot(leave[...], flat, preferred_element_type=jnp.float32).astype(jnp.bfloat16)


def other_core_part(leave, rows, after):
    slot_count, held_rows, width = rows.shape
    units, held = leave.shape
    tile = tile_of(width)
    return pl.pallas_call(
        part_kernel,
        grid=(width // tile,),
        in_specs=[
            pl.BlockSpec((units, held), lambda j: (0, 0)),
            pl.BlockSpec((slot_count, held_rows, tile), lambda j: (0, 0, j)),
        ]
        + [pl.BlockSpec(memory_space=pl.ANY)] * len(after),
        out_specs=pl.BlockSpec((units, tile), lambda j: (0, j)),
        out_shape=jax.ShapeDtypeStruct((units, width), jnp.bfloat16),
        cost_estimate=cost(2 * units * held * width),
    )(leave, rows, *after)


def near_kernel(chips, stay, rows, near, *rest):
    mine, *others = rest[-chips:]
    flat = rows[...].reshape(-1, rows.shape[-1])
    shard = mine.shape[0]
    total = jnp.dot(stay[...], flat, preferred_element_type=jnp.float32) + near[...].astype(jnp.float32)
    mine[...] = total[:shard]
    for d, other in enumerate(others):
        other[...] = total[(d + 1) * shard : (d + 2) * shard].astype(jnp.bfloat16)


def add_near(stay, rows, near, chips, after):
    units, held = stay.shape
    width = rows.shape[-1]
    shard = units // chips
    tile = tile_of(width)
    return pl.pallas_call(
        functools.partial(near_kernel, chips),
        grid=(width // tile,),
        in_specs=[
            pl.BlockSpec((units, held), lambda j: (0, 0)),
            pl.BlockSpec(rows.shape[:2] + (tile,), lambda j: (0, 0, j)),
            pl.BlockSpec((units, tile), lambda j: (0, j)),
        ]
        + [pl.BlockSpec(memory_space=pl.ANY)] * len(after),
        out_specs=(pl.BlockSpec((shard, tile), lambda j: (0, j)),) * chips,
        out_shape=(jax.ShapeDtypeStruct((shard, width), jnp.float32),)
        + (jax.ShapeDtypeStruct((shard, width), jnp.bfloat16),) * (chips - 1),
        cost_estimate=cost(2 * units * held * width),
    )(stay, rows, near, *after)


def hold_kernel(*refs):
    pass


def hold(array, after):
    return pl.pallas_call(
        hold_kernel,
        in_specs=[pl.BlockSpec(memory_space=pl.ANY)] * (1 + len(after)),
        out_specs=pl.BlockSpec(memory_space=pl.ANY),
        out_shape=jax.ShapeDtypeStruct(array.shape, array.dtype),
        input_output_aliases={0: 0},
        cost_estimate=cost(1),
    )(array, *after)


def return_kernel(score, rank, slot_of, gates, out):
    slot_count, cap_rows = score.shape
    top_count, tokens = slot_of.shape
    row_ids = lax.broadcasted_iota(jnp.int32, (cap_rows, tokens), 0)
    total = jnp.zeros((top_count, tokens), jnp.float32)
    for s in range(slot_count):
        onehot = jnp.where(row_ids == rank[s : s + 1, :], 1.0, 0.0)
        value = lax.dot_general(
            score[s : s + 1, :],
            onehot,
            (((1,), (0,)), ((), ())),
            precision=lax.Precision.HIGHEST,
            preferred_element_type=jnp.float32,
        )
        total = jnp.where(slot_of[...] == s, value, total)
    held_gate = gates[...].astype(jnp.bfloat16).astype(jnp.float32)
    out[...] = jnp.where(slot_of[...] >= 0, total / held_gate, 0.0)


def matchings(slot_count):
    first = np.zeros((1 << slot_count,), np.int32)
    perms = []
    for four in itertools.combinations(range(slot_count), 4):
        first[sum(1 << s for s in four)] = len(perms)
        for other in range(3):
            rest = [four[1 + i] for i in range(3) if i != other]
            pairs = ((four[0], four[1 + other]), tuple(rest))
            perms.append([(a, b) for a, b in pairs] + [(b, a) for a, b in pairs])
    return first, perms


def matching_index(replica_plan, first):
    slot_ids, same_expert, ordinal = slot_layout(replica_plan)
    hot = jnp.sum(same_expert, axis=1) > 1
    mask = jnp.sum(jnp.where(hot, 1 << slot_ids, 0))
    least = jnp.min(jnp.where(hot, slot_ids, slot_ids.shape[0]))
    expert = jnp.sum(jnp.where(slot_ids == least, replica_plan, 0))
    partner = jnp.max(jnp.where(replica_plan == expert, slot_ids, 0))
    between = jnp.sum(hot & (slot_ids > least) & (slot_ids < partner))
    base = jnp.sum(jnp.where(jnp.arange(first.shape[0]) == mask, jnp.asarray(first), 0))
    return base + between


def sum_copies_any(group_sum, replica_plan):
    slot_ids, same_expert, ordinal = slot_layout(replica_plan)
    copies = jnp.sum(same_expert, axis=1)
    hot_first = (copies > 1) & (ordinal == 0)
    hot_rank = jnp.sum(hot_first[None, :] & (replica_plan[None, :] < replica_plan[:, None]), axis=1)
    my_slot = slot_ids == lax.axis_index("expert")
    my_rank = jnp.sum(jnp.where(my_slot, hot_rank, 0))
    my_hot = jnp.any(my_slot & (copies > 1))
    place_hot = (jnp.arange(HOT, dtype=jnp.int32) == my_rank) & my_hot
    group_f = group_sum.astype(jnp.float32)
    table = jnp.where(place_hot[:, None, None], group_f[None], 0.0)
    summed = lax.psum(table.astype(jnp.bfloat16), "expert").astype(jnp.float32)
    picked = jnp.sum(jnp.where(place_hot[:, None, None], summed, 0.0), axis=0)
    return jnp.where(my_hot, picked, group_f).astype(jnp.bfloat16)


def local(out_grad, gates, routes, copy_pick, replica_plan, down_weight, saved_hidden):
    slot_count = replica_plan.shape[0]
    cap_rows = saved_hidden.shape[3]
    expert_count = slot_count - slot_count // 4
    model_width = out_grad.shape[1]
    hidden_units = down_weight.shape[1]
    group_size = lax.axis_size("group")
    chips = group_size // 2
    shard_rows = hidden_units // group_size
    me = lax.axis_index("group")
    chip, core = me // 2, me % 2

    seat = lax.axis_index("expert").astype(jnp.int32).reshape(1)
    held_rows = -(-cap_rows // 16) * 16
    pad = ((0, 0), (0, held_rows - cap_rows), (0, 0))
    held_hidden = jnp.pad(saved_hidden[0, 0], pad).reshape(slot_count * held_rows, hidden_units)

    spread, rank, slot_of = place_routes(
        routes.T, copy_pick.T, gates.T, replica_plan, seat, expert_count, cap_rows, held_rows
    )

    by_owner = held_hidden.T.reshape(chips, 2, shard_rows, -1)
    by_owner = jnp.stack([by_owner[chip ^ d] for d in range(chips)])
    stay = by_owner[:, core].reshape(hidden_units // 2, -1)
    leave = by_owner[:, 1 - core].reshape(hidden_units // 2, -1)

    edges = np.cumsum((0,) + CHUNKS)
    spans = [(int(a), int(b)) for a, b in zip(edges[:-1], edges[1:])]
    ready = [all_rows_to_send(spread, out_grad, seat, span, []) for span in spans]
    pairs = slot_count - expert_count == HOT
    if pairs:
        first, perms = matchings(slot_count)
        pairing = matching_index(replica_plan, first)
    group_sum, projected = [], jnp.zeros((slot_count * held_rows, hidden_units), jnp.float32)
    rows, far, others = None, [], []
    early = ready[2:] + ([pairing.reshape(1)] if pairs else [])
    for span, sent in zip(spans, ready):
        if rows is not None:
            sent = hold(sent, [rows] + early)
            early = others[:1] + [projected]
        rows = lax.all_to_all(sent, "expert", split_axis=0, concat_axis=0, tiled=True)
        away = other_core_part(leave, rows, others[:1])
        near = lax.ppermute(away, "group", [(i, i ^ 1) for i in range(group_size)])
        mine, *others = add_near(stay, rows, near, chips, far[:1])
        far = [
            lax.ppermute(other, "group", [(i, i ^ (2 * d + 2)) for i in range(group_size)])
            for d, other in enumerate(others)
        ]
        group_sum.append(sum((f.astype(jnp.float32) for f in far), mine).astype(jnp.bfloat16))
        projected = projected + lax.dot_general(
            rows.reshape(slot_count * held_rows, -1),
            down_weight[0, :, span[0] : span[1]],
            (((1,), (1,)), ((), ())),
            preferred_element_type=jnp.float32,
        )

    route_score = jnp.sum(projected * held_hidden.astype(jnp.float32), axis=1)
    returned = lax.all_to_all(
        hold(route_score.reshape(slot_count, held_rows), others[:1]),
        "expert",
        split_axis=0,
        concat_axis=0,
        tiled=True,
    )
    route_grad = pl.pallas_call(
        return_kernel, out_shape=jax.ShapeDtypeStruct(gates.T.shape, jnp.float32)
    )(returned, rank, slot_of, gates.T).T
    hidden_grad = projected.astype(jnp.bfloat16).reshape(slot_count, held_rows, hidden_units)[:, :cap_rows]

    group_sum = jnp.concatenate(group_sum, axis=1)
    if pairs:
        other = lax.switch(
            pairing,
            [functools.partial(lax.ppermute, axis_name="expert", perm=perm) for perm in perms],
            group_sum,
        )
        copy_grad = (group_sum.astype(jnp.float32) + other.astype(jnp.float32)).astype(jnp.bfloat16)
    else:
        copy_grad = sum_copies_any(group_sum, replica_plan)
    return (route_grad, hidden_grad[None, None], copy_grad.reshape(1, shard_rows, model_width))


def solution(mesh):
    placed = (
        P(("group", "expert"), None),
        P(("group", "expert"), None),
        P(("group", "expert"), None),
        P(("group", "expert"), None),
        P(),
        P("expert", None, None),
        P("group", "expert", None, None, None),
    )
    return jax.shard_map(
        local,
        mesh=mesh,
        in_specs=placed,
        out_specs=(
            P(("group", "expert"), None),
            P("group", "expert", None, None, None),
            P("expert", "group", None),
        ),
        check_vma=False,
    )
```

profile of v0, /device:TPU:0, one launch (start us, length us, event | category | flops | bytes accessed | tf_op | source)
XLA Modules:
  0.0 210.4 jit_solution(9263013428140271699)
XLA Ops:
  0.6 1.9 shard_map.103
  2.5 4.5 %shard_map.104 = bf16[8,80,2048]{2,1,0:T(8,128)(2,1)} custom-call(s32[1]{0:T(128)} %bitcast.seat, bf16[8,80,256]{2,1,0:T(8,128)(2,1)} %get-tuple-element.439.spread, bf16[256,3584]{1,0:T(8,128)(2,1)} %rows.5), custom_call_target="tpu_custom_call" | custom-call | flops 671088640 | bytes 2236962 | tf_op jit(solution)/shard_map/pallas_call | solution.py:110
  7.0 7.3 %all-to-all-start = ((bf16[8,80,2048]{2,1,0:T(8,128)(2,1)}), bf16[8,80,2048]{2,1,0:T(8,128)(2,1)S(1)}, u32[]{:S(2)}, u32[]{:S(2)}) async-start(bf16[8,80,2048]{2,1,0:T(8,128)(2,1)} %shard_map.104), calls=%async_computation | async-start | bytes 5242880 | tf_op jit(solution)/shard_map/all_to_all | solution.py:293
  14.3 4.4 %reshape.47 = bf16[2,2,256,640]{2,1,0,3:T(2,128)(2,1)} reshape(bf16[1024,640]{0,1:T(8,128)(2,1)} %bitcast.47) | data formatting | bytes 2621440 | tf_op jit(solution)/shard_map/reshape | solution.py:274
  18.6 3.3 %constant_dynamic-slice_fusion = (bf16[1,2,256,640]{2,1,0,3:T(2,128)(2,1)}, bf16[1,2,256,640]{2,1,0,3:T(2,128)(2,1)}) fusion(bf16[2,2,256,640]{2,1,0,3:T(2,128)(2,1)} %reshape.47, s32[]{:T(128)S(6)} %select_n.47, s32[]{:T(128)S(6)} %select_n.46), kind=kLoop, calls=%fused_computation.27 | loop fusion | bytes 2621448 | tf_op jit(solution)/shard_map/dynamic_slice | solution.py:275
  21.9 2.3 %copy.23 = bf16[1,2,256,640]{3,2,0,1:T(8,128)(2,1)S(1)} copy(bf16[1,2,256,640]{2,1,0,3:T(2,128)(2,1)} %get-tuple-element.454) | data formatting | bytes 1310720
  24.2 2.9 %copy.22 = bf16[1,2,256,640]{3,2,0,1:T(8,128)(2,1)} copy(bf16[1,2,256,640]{2,1,0,3:T(2,128)(2,1)} %get-tuple-element.455) | data formatting | bytes 1310720
  27.1 0.0 copy-done.12
  27.1 0.2 convert_reduce_fusion
  27.3 0.6 select_reduce_fusion
  28.0 1.3 fusion.12
  29.3 1.3 fusion.13
  30.5 1.9 fusion.14
  32.4 0.0 copy-done.13
  32.4 1.3 fusion.11
  35.0 2.2 %shard_map.106.refs_2_.refs_0_ = bf16[8,80,512]{2,1,0:T(8,128)(2,1)} custom-call(s32[1]{0:T(128)} %bitcast.seat, bf16[8,80,256]{2,1,0:T(8,128)(2,1)} %get-tuple-element.439.spread, bf16[256,3584]{1,0:T(8,128)(2,1)} %rows.5), custom_call_target="tpu_custom_call" | custom-call | flops 167772160 | bytes 559240 | tf_op jit(solution)/shard_map/pallas_call | solution.py:110
  37.2 2.6 %shard_map.105.refs_0_ = bf16[8,80,1024]{2,1,0:T(8,128)(2,1)} custom-call(s32[1]{0:T(128)} %bitcast.seat, bf16[8,80,256]{2,1,0:T(8,128)(2,1)} %get-tuple-element.439.spread, bf16[256,3584]{1,0:T(8,128)(2,1)} %rows.5), custom_call_target="tpu_custom_call" | custom-call | flops 335544320 | bytes 1118481 | tf_op jit(solution)/shard_map/pallas_call | solution.py:110
  39.8 2.3 %fusion.9 = (bf16[2,1,256,640]{3,2,0,1:T(8,128)(2,1)}, bf16[2,1,256,640]{3,2,0,1:T(8,128)(2,1)}) fusion(s32[]{:T(128)S(6)} %select_n.50, bf16[1,2,256,640]{3,2,0,1:T(8,128)(2,1)} %copy.22, bf16[1,2,256,640]{3,2,0,1:T(8,128)(2,1)S(1)} %copy.23, s32[]{:T(128)S(6)} %select_n.49), kind=kLoop, calls=%fused_computation.19 | loop fusion | flops 655360 | bytes 2621448 | tf_op jit(solution)/shard_map/stack | solution.py:275
  42.1 31.7 %all-to-all-done.refs_1_.rows = bf16[8,80,2048]{2,1,0:T(8,128)(2,1)S(1)} async-done(((bf16[8,80,2048]{2,1,0:T(8,128)(2,1)}), bf16[8,80,2048]{2,1,0:T(8,128)(2,1)S(1)}, u32[]{:S(2)}, u32[]{:S(2)}) %all-to-all-start) | async-done | bytes 2621472 | tf_op jit(solution)/shard_map/all_to_all | solution.py:293
  73.7 1.5 copy-done
  75.3 4.3 %all-to-all-start.1 = ((bf16[8,80,1024]{2,1,0:T(8,128)(2,1)}), bf16[8,80,1024]{2,1,0:T(8,128)(2,1)}, u32[]{:S(2)}, u32[]{:S(2)}) async-start(bf16[8,80,1024]{2,1,0:T(8,128)(2,1)} %shard_map.107), calls=%async_computation.1 | async-start | bytes 2621440 | tf_op jit(solution)/shard_map/all_to_all | solution.py:293
  79.6 0.0 copy-start.1
  79.6 5.4 %shard_map.108 = bf16[512,2048]{1,0:T(8,128)(2,1)} custom-call(bf16[512,640]{1,0:T(8,128)(2,1)} %bitcast.44, bf16[8,80,2048]{2,1,0:T(8,128)(2,1)} %copy-done), custom_call_target="tpu_custom_call" | custom-call | flops 1342177280 | bytes 4473924 | tf_op jit(solution)/shard_map/pallas_call | solution.py:134
  85.0 0.0 collective-permute-start.210
  85.0 0.0 copy-done.1
  85.0 6.6 %fusion.refs_3_ = f32[640,1024]{1,0:T(8,128)} fusion(bf16[640,2048]{1,0:T(8,128)(2,1)S(1)} %bitcast.39, bf16[1,1024,3584]{2,1,0:T(8,128)(2,1)} %param.223), kind=kOutput, calls=%fused_computation | convolution fusion | flops 2684354560 | bytes 9437184 | tf_op jit(solution)/shard_map/dot_general | solution.py:302
  91.6 0.0 collective-permute-done.210.near
  91.6 5.6 %shard_map.109 = (f32[256,2048]{1,0:T(8,128)}, bf16[256,2048]{1,0:T(8,128)(2,1)}) custom-call(bf16[512,640]{1,0:T(8,128)(2,1)} %bitcast.41, bf16[8,80,2048]{2,1,0:T(8,128)(2,1)} %copy-done, bf16[512,2048]{1,0:T(8,128)(2,1)} %collective-permute-done.210.near), custom_call_target="tpu_custom_call" | custom-call | flops 1342177280 | bytes 4473924 | tf_op jit(solution)/shard_map/pallas_call | solution.py:163
  97.2 1.5 collective-permute-start.212
  98.7 11.9 %all-to-all-done.1.refs_1_.rows = bf16[8,80,1024]{2,1,0:T(8,128)(2,1)} async-done(((bf16[8,80,1024]{2,1,0:T(8,128)(2,1)}), bf16[8,80,1024]{2,1,0:T(8,128)(2,1)}, u32[]{:S(2)}, u32[]{:S(2)}) %all-to-all-start.1) | async-done | bytes 1310752 | tf_op jit(solution)/shard_map/all_to_all | solution.py:293
  110.6 3.7 %all-to-all-start.2 = ((bf16[8,80,512]{2,1,0:T(8,128)(2,1)}), bf16[8,80,512]{2,1,0:T(8,128)(2,1)S(1)}, u32[]{:S(2)}, u32[]{:S(2)}) async-start(bf16[8,80,512]{2,1,0:T(8,128)(2,1)} %shard_map.110), calls=%async_computation.2 | async-start | bytes 1310720 | tf_op jit(solution)/shard_map/all_to_all | solution.py:293
  114.4 3.3 %shard_map.111 = bf16[512,1024]{1,0:T(8,128)(2,1)} custom-call(bf16[512,640]{1,0:T(8,128)(2,1)} %bitcast.45, bf16[8,80,1024]{2,1,0:T(8,128)(2,1)} %all-to-all-done.1.refs_1_.rows, bf16[256,2048]{1,0:T(8,128)(2,1)} %get-tuple-element.440.refs_2_.rest_0_), custom_call_target="tpu_custom_call" | custom-call | flops 671088640 | bytes 2236962 | tf_op jit(solution)/shard_map/pallas_call | solution.py:134
  117.6 0.0 collective-permute-start.211
  117.6 5.1 %fusion.3 = f32[640,1024]{1,0:T(8,128)} fusion(bf16[640,1024]{1,0:T(8,128)(2,1)} %bitcast.8, bf16[1,1024,3584]{2,1,0:T(8,128)(2,1)} %param.223), kind=kOutput, calls=%fused_computation.6 | convolution fusion | flops 1342177280 | bytes 6029312 | tf_op jit(solution)/shard_map/dot_general | solution.py:302
  122.7 0.3 collective-permute-done.212.rest_0_
  123.0 0.0 collective-permute-done.211.near
  123.0 1.0 copy-done.6
  124.0 1.0 copy-done.9
  125.0 3.5 %shard_map.112 = (f32[256,1024]{1,0:T(8,128)}, bf16[256,1024]{1,0:T(8,128)(2,1)}) custom-call(bf16[512,640]{1,0:T(8,128)(2,1)} %bitcast.42, bf16[8,80,1024]{2,1,0:T(8,128)(2,1)} %all-to-all-done.1.refs_1_.rows, bf16[512,1024]{1,0:T(8,128)(2,1)} %copy-done.9, bf16[256,2048]{1,0:T(8,128)(2,1)} %copy-done.6), custom_call_target="tpu_custom_call" | custom-call | flops 671088640 | bytes 2236962 | tf_op jit(solution)/shard_map/pallas_call | solution.py:163
  128.4 1.5 collective-permute-start.214
  129.9 1.7 all-to-all-done.2.rows
  131.7 0.8 copy-done.2
  132.5 2.8 %shard_map.113 = bf16[512,512]{1,0:T(8,128)(2,1)} custom-call(bf16[512,640]{1,0:T(8,128)(2,1)} %bitcast.46, bf16[8,80,512]{2,1,0:T(8,128)(2,1)} %copy-done.2, bf16[256,1024]{1,0:T(8,128)(2,1)} %get-tuple-element.441.rest_0_), custom_call_target="tpu_custom_call" | custom-call | flops 335544320 | bytes 1118481 | tf_op jit(solution)/shard_map/pallas_call | solution.py:134
  135.3 0.0 collective-permute-start.213
  135.3 2.0 add_convert_fusion.1
  137.4 0.5 copy-done.4
  137.9 4.3 %fusion.15 = (bf16[640,1024]{1,0:T(8,128)(2,1)}, f32[640]{0:T(1024)S(1)}) fusion(bf16[1,1,8,80,1024]{4,3,2,1,0:T(8,128)(2,1)S(1)} %copy-done.5, bf16[640,512]{1,0:T(8,128)(2,1)S(1)} %bitcast.40, bf16[1,1024,3584]{2,1,0:T(8,128)(2,1)} %param.223, f32[640,1024]{1,0:T(8,128)S(1)} %copy-done.4, f32[640,1024]{1,0:T(8,128)} %fusion.3), kind=kOutput, calls=%fused_computation.36 | convolution fusion | flops 675020160 | bytes 9570816 | tf_op jit(solution)/shard_map/dot_general | solution.py:302
  142.2 0.7 reshape.49.refs_0_
  142.9 0.0 collective-permute-done.214.rest_0_
  142.9 0.0 collective-permute-done.213.near
  142.9 2.8 %shard_map.114 = (f32[256,512]{1,0:T(8,128)}, bf16[256,512]{1,0:T(8,128)(2,1)}) custom-call(bf16[512,640]{1,0:T(8,128)(2,1)} %bitcast.43, bf16[8,80,512]{2,1,0:T(8,128)(2,1)} %copy-done.2, bf16[512,512]{1,0:T(8,128)(2,1)} %collective-permute-done.213.near, bf16[256,1024]{1,0:T(8,128)(2,1)} %collective-permute-done.214.rest_0_), custom_call_target="tpu_custom_call" | custom-call | flops 335544320 | bytes 1118481 | tf_op jit(solution)/shard_map/pallas_call | solution.py:163
  145.7 1.5 collective-permute-start.215
  147.2 5.7 %all-to-all-start.3 = ((f32[8,1,80]{2,1,0:T(1,128)}), f32[8,1,80]{2,1,0:T(1,128)S(1)}, u32[]{:S(2)}, u32[]{:S(2)}) async-start(f32[8,1,80]{2,1,0:T(1,128)} %bitcast.49), calls=%async_computation.3 | async-start | bytes 8192 | tf_op jit(solution)/shard_map/all_to_all | solution.py:310
  152.9 1.2 add_convert_fusion.2
  154.1 5.2 %all-to-all-done.3 = f32[8,1,80]{2,1,0:T(1,128)S(1)} async-done(((f32[8,1,80]{2,1,0:T(1,128)}), f32[8,1,80]{2,1,0:T(1,128)S(1)}, u32[]{:S(2)}, u32[]{:S(2)}) %all-to-all-start.3) | async-done | bytes 2592 | tf_op jit(solution)/shard_map/all_to_all | solution.py:310
  159.3 0.6 copy-done.11
  159.9 1.8 shard_map.116
  161.7 0.0 collective-permute-done.215
  161.7 0.1 add_convert_fusion.3
  161.8 0.1 pad_maximum_fusion
  161.9 45.2 %conditional.4 = (bf16[256,3584]{1,0:T(8,128)(2,1)}) conditional(s32[]{:T(128)} %clamp.3, bf16[256,3584]{1,0:T(8,128)(2,1)S(1)} %pad_maximum_fusion, bf16[256,3584]{1,0:T(8,128)(2,1)S(1)} %pad_maximum_fusion, bf16[256,3584]{1,0:T(8,128)(2,1)S(1)} %pad_maximum_fusion, ...), branch_computations={%region_8.9_spmd, %region_9.10_spmd, %region_10.11_spmd, %region_1... | conditional | bytes 7340080
  161.9 2.0 collective-permute-start.55
  163.9 43.2 %collective-permute-done.55 = bf16[256,3584]{1,0:T(8,128)(2,1)} collective-permute-done((bf16[256,3584]{1,0:T(8,128)(2,1)S(1)}, bf16[256,3584]{1,0:T(8,128)(2,1)}, u32[]{:S(2)}, u32[]{:S(2)}) %collective-permute-start.55) | collective-permute-done | bytes 1835040 | tf_op jit(solution)/shard_map/cond/branch_55_fun/ppermute | solution.py:324
  207.1 3.2 %fusion.6 = bf16[1,256,3584]{2,1,0:T(8,128)(2,1)} fusion(bf16[256,3584]{1,0:T(8,128)(2,1)} %get-tuple-element.456, bf16[256,512]{1,0:T(8,128)(2,1)S(1)} %add_convert_fusion.3, bf16[256,1024]{1,0:T(8,128)(2,1)S(1)} %add_convert_fusion.2, bf16[256,2048]{1,0:T(8,128)(2,1)S(1)} %add_convert_fusion.1), kind=kLoop, calls=%fused_computation.10 | loop fusion | flops 8257536 | bytes 5505024 | tf_op jit(solution)/shard_map/reshape | solution.py:332
  (21 shorter events, 0.0 us)
Async XLA Ops:
  7.0 66.8 %all-to-all-start = ((bf16[8,80,2048]{2,1,0:T(8,128)(2,1)}), bf16[8,80,2048]{2,1,0:T(8,128)(2,1)S(1)}, u32[]{:S(2)}, u32[]{:S(2)}) async-start(bf16[8,80,2048]{2,1,0:T(8,128)(2,1)} %shard_map.104), calls=%async_computation | async-start | bytes 5242880 | tf_op jit(solution)/shard_map/all_to_all | solution.py:293
  21.9 5.2 %copy-start.12 = (s32[8]{0:T(128)S(1)}, s32[8]{0:T(128)}, u32[]{:S(2)}) copy-start(s32[8]{0:T(128)} %slot_plan.1) | copy-start | bytes 100
  21.9 10.6 %copy-start.13 = (s32[256]{0:T(256)S(1)}, s32[256]{0:T(256)}, u32[]{:S(2)}) copy-start(s32[256]{0:T(256)} %constant.49.clone) | copy-start | bytes 3076
  73.7 1.5 copy-start
  75.3 35.3 %all-to-all-start.1 = ((bf16[8,80,1024]{2,1,0:T(8,128)(2,1)}), bf16[8,80,1024]{2,1,0:T(8,128)(2,1)}, u32[]{:S(2)}, u32[]{:S(2)}) async-start(bf16[8,80,1024]{2,1,0:T(8,128)(2,1)} %shard_map.107), calls=%async_computation.1 | async-start | bytes 2621440 | tf_op jit(solution)/shard_map/all_to_all | solution.py:293
  79.6 5.4 %copy-start.1 = (bf16[8,80,2048]{2,1,0:T(8,128)(2,1)S(1)}, bf16[8,80,2048]{2,1,0:T(8,128)(2,1)}, u32[]{:S(2)}) copy-start(bf16[8,80,2048]{2,1,0:T(8,128)(2,1)} %copy-done) | copy-start | bytes 7864324
  85.0 6.6 %collective-permute-start.210 = (bf16[512,2048]{1,0:T(8,128)(2,1)}, bf16[512,2048]{1,0:T(8,128)(2,1)}, u32[]{:S(2)}, u32[]{:S(2)}) collective-permute-start(bf16[512,2048]{1,0:T(8,128)(2,1)} %shard_map.108), channel_id=1, source_target_pairs={{0,8},{8,0},{16,24},{24,16},{1,9},{9,1},{17,25},{25,17},{2,10},{10... | collective-permute-start | bytes 6291464 | tf_op jit(solution)/shard_map/ppermute | solution.py:295
  97.2 25.8 %collective-permute-start.212 = (bf16[256,2048]{1,0:T(8,128)(2,1)}, bf16[256,2048]{1,0:T(8,128)(2,1)S(1)}, u32[]{:S(2)}, u32[]{:S(2)}) collective-permute-start(bf16[256,2048]{1,0:T(8,128)(2,1)} %get-tuple-element.440.refs_2_.rest_0_), channel_id=1, source_target_pairs={{0,16},{8,24},{16,0},{24,8},{1,17},{9,25},{17,1},{25,9},{2,18},{10... | collective-permute-start | bytes 3145736 | tf_op jit(solution)/shard_map/ppermute | solution.py:298
  110.6 21.0 %all-to-all-start.2 = ((bf16[8,80,512]{2,1,0:T(8,128)(2,1)}), bf16[8,80,512]{2,1,0:T(8,128)(2,1)S(1)}, u32[]{:S(2)}, u32[]{:S(2)}) async-start(bf16[8,80,512]{2,1,0:T(8,128)(2,1)} %shard_map.110), calls=%async_computation.2 | async-start | bytes 1310720 | tf_op jit(solution)/shard_map/all_to_all | solution.py:293
  117.6 5.4 %collective-permute-start.211 = (bf16[512,1024]{1,0:T(8,128)(2,1)}, bf16[512,1024]{1,0:T(8,128)(2,1)S(1)}, u32[]{:S(2)}, u32[]{:S(2)}) collective-permute-start(bf16[512,1024]{1,0:T(8,128)(2,1)} %shard_map.111), channel_id=1, source_target_pairs={{0,8},{8,0},{16,24},{24,16},{1,9},{9,1},{17,25},{25,17},{2,10},{10... | collective-permute-start | bytes 3145736 | tf_op jit(solution)/shard_map/ppermute | solution.py:295
  123.0 1.0 copy-start.6
  124.0 1.0 copy-start.9
  128.4 6.8 %copy-start.7 = (bf16[256,2048]{1,0:T(8,128)(2,1)S(1)}, bf16[256,2048]{1,0:T(8,128)(2,1)}, u32[]{:S(2)}) copy-start(bf16[256,2048]{1,0:T(8,128)(2,1)} %copy-done.6) | copy-start | bytes 3145732
  128.4 14.4 %collective-permute-start.214 = (bf16[256,1024]{1,0:T(8,128)(2,1)}, bf16[256,1024]{1,0:T(8,128)(2,1)}, u32[]{:S(2)}, u32[]{:S(2)}) collective-permute-start(bf16[256,1024]{1,0:T(8,128)(2,1)} %get-tuple-element.441.rest_0_), channel_id=1, source_target_pairs={{0,16},{8,24},{16,0},{24,8},{1,17},{9,25},{17,1},{25,9},{2,18},{10... | collective-permute-start | bytes 1572872 | tf_op jit(solution)/shard_map/ppermute | solution.py:298
  131.7 0.9 copy-start.2
  132.5 4.8 %copy-start.5 = (bf16[1,1,8,80,1024]{4,3,2,1,0:T(8,128)(2,1)S(1)}, bf16[1,1,8,80,1024]{4,3,2,1,0:T(8,128)(2,1)}, u32[]{:S(2)}) copy-start(bf16[1,1,8,80,1024]{4,3,2,1,0:T(8,128)(2,1)} %param.224) | copy-start | bytes 3932164
  135.3 7.6 %collective-permute-start.213 = (bf16[512,512]{1,0:T(8,128)(2,1)}, bf16[512,512]{1,0:T(8,128)(2,1)}, u32[]{:S(2)}, u32[]{:S(2)}) collective-permute-start(bf16[512,512]{1,0:T(8,128)(2,1)} %shard_map.113), channel_id=1, source_target_pairs={{0,8},{8,0},{16,24},{24,16},{1,9},{9,1},{17,25},{25,17},{2,10},{10... | collective-permute-start | bytes 1572872 | tf_op jit(solution)/shard_map/ppermute | solution.py:295
  135.3 2.1 copy-start.3
  135.3 2.6 %copy-start.4 = (f32[640,1024]{1,0:T(8,128)S(1)}, f32[640,1024]{1,0:T(8,128)}, u32[]{:S(2)}) copy-start(f32[640,1024]{1,0:T(8,128)} %fusion.refs_3_) | copy-start | bytes 7864324
  142.2 10.7 %copy-start.8 = (f32[256,1024]{1,0:T(8,128)S(1)}, f32[256,1024]{1,0:T(8,128)}, u32[]{:S(2)}) copy-start(f32[256,1024]{1,0:T(8,128)} %get-tuple-element.446) | copy-start | bytes 3145732
  145.7 16.0 %copy-start.10 = (f32[256,512]{1,0:T(8,128)S(1)}, f32[256,512]{1,0:T(8,128)}, u32[]{:S(2)}) copy-start(f32[256,512]{1,0:T(8,128)} %get-tuple-element.447) | copy-start | bytes 1572868
  145.7 16.0 %collective-permute-start.215 = (bf16[256,512]{1,0:T(8,128)(2,1)}, bf16[256,512]{1,0:T(8,128)(2,1)S(1)}, u32[]{:S(2)}, u32[]{:S(2)}) collective-permute-start(bf16[256,512]{1,0:T(8,128)(2,1)} %get-tuple-element.442.refs_1_), channel_id=1, source_target_pairs={{0,16},{8,24},{16,0},{24,8},{1,17},{9,25},{17,1},{25,9},{2,18},{10... | collective-permute-start | bytes 786440 | tf_op jit(solution)/shard_map/ppermute | solution.py:298
  147.2 12.1 %all-to-all-start.3 = ((f32[8,1,80]{2,1,0:T(1,128)}), f32[8,1,80]{2,1,0:T(1,128)S(1)}, u32[]{:S(2)}, u32[]{:S(2)}) async-start(f32[8,1,80]{2,1,0:T(1,128)} %bitcast.49), calls=%async_computation.3 | async-start | bytes 8192 | tf_op jit(solution)/shard_map/all_to_all | solution.py:310
  159.3 0.6 copy-start.11
  161.9 45.2 %collective-permute-start.55 = (bf16[256,3584]{1,0:T(8,128)(2,1)S(1)}, bf16[256,3584]{1,0:T(8,128)(2,1)}, u32[]{:S(2)}, u32[]{:S(2)}) collective-permute-start(bf16[256,3584]{1,0:T(8,128)(2,1)S(1)} %param.55), channel_id=1, source_target_pairs={{0,3},{2,7},{3,0},{7,2},{8,11},{10,15},{11,8},{15,10},{16,19},{18,... | collective-permute-start | bytes 5505032 | tf_op jit(solution)/shard_map/cond/branch_55_fun/ppermute | solution.py:324
where the time goes:
time: 213 us; the launch traced here: 210 us
  waiting for transfers between devices  94 us (44%)
  Pallas kernels  36.3 us (17%)
  starting transfers between devices  27.5 us (13%)
  local copies, waits for them, and re-layouts  19 us (9%)
  matrix products  16 us (8%)
  other arithmetic  15.5 us (7%)
    all_to_all x3, waiting for transfers between devices, local(): lax.all_to_all(sent, 'expert', split_axis=0, concat_axis=0, tiled=True)  45.3 us
    ppermute x1, waiting for transfers between devices, local(): lax.switch(pairing, [functools.partial(lax.ppermute, axis_name='expert',...  43.2 us
    dot_general x3, matrix products, local(): lax.dot_general(rows.reshape(slot_count * held_rows, -1), down_weight[0,...  16 us
    all_to_all x3, starting transfers between devices, local(): lax.all_to_all(sent, 'expert', split_axis=0, concat_axis=0, tiled=True)  15.3 us
    pallas_call x3, Pallas kernels, add_near(): pl.pallas_call(functools.partial(near_kernel, chips), grid=(width // tile...  11.9 us
    pallas_call x3, Pallas kernels, other_core_part(): pl.pallas_call(part_kernel, grid=(width // tile,), in_specs=[pl.BlockSpec...  11.4 us
    unnamed x30, local copies, waits for them, and re-layouts  10.7 us
    pallas_call x3, Pallas kernels, all_rows_to_send(): pl.pallas_call(send_all_kernel, grid=((stop - start) // tile,), in_specs=...  9.24 us
  transfers between devices with their start and end apart: 11, of which 6 were waited for; matrix products, arithmetic and copies ran while one was open for 20% of the time, Pallas kernels for 13%

commit v1 on v0

--- a/solution.py
+++ b/solution.py
@@ -10,16 +10,12 @@
 from jax.sharding import PartitionSpec as P
 
 HOT = 2
-tile = 512
-
-
-def tile_of(width, start=0):
-    return next(t for t in (512, 896, 640, 384, 256, 128, width) if width % t == 0 and start % t == 0)
 
 
 def cost(flops):
     return pl.CostEstimate(flops=flops, bytes_accessed=flops // 300, transcendentals=0)
-CHUNKS = (2048, 1024, 512)
+CHUNKS = (2048, 896, 640)
+VMEM_BYTES = 32 * 1024 * 1024
 
 
 def slot_layout(replica_plan):
@@ -106,7 +102,7 @@
 def all_rows_to_send(spread, out_grad, seat, span, after):
     slot_count, held_rows, tokens = spread.shape
     start, stop = span
-    tile = tile_of(stop - start, start)
+    tile = next(t for t in (512, 256, 128) if start % t == 0 and stop % t == 0)
     return pl.pallas_call(
         send_all_kernel,
         grid=((stop - start) // tile,),
@@ -122,62 +118,72 @@
     )(seat, spread, out_grad, *after)
 
 
+def columns(body, width):
+    tile = 512 if width % 512 == 0 else width
+
+    @pl.loop(0, width // tile)
+    def _(j):
+        body(pl.ds(pl.multiple_of(j * tile, tile), tile))
+
+
 def part_kernel(leave, rows, *rest):
-    flat = rows[...].reshape(-1, rows.shape[-1])
-    rest[-1][...] = jnp.dot(leave[...], flat, preferred_element_type=jnp.float32).astype(jnp.bfloat16)
+    def some(at):
+        flat = rows[:, :, at].reshape(leave.shape[1], -1)
+        rest[-1][:, at] = jnp.dot(leave[...], flat, preferred_element_type=jnp.float32).astype(jnp.bfloat16)
+
+    columns(some, rows.shape[-1])
 
 
 def other_core_part(leave, rows, after):
-    slot_count, held_rows, width = rows.shape
+    width = rows.shape[-1]
     units, held = leave.shape
-    tile = tile_of(width)
+    vmem = pl.BlockSpec(memory_space=pltpu.VMEM)
     return pl.pallas_call(
         part_kernel,
-        grid=(width // tile,),
-        in_specs=[
-            pl.BlockSpec((units, held), lambda j: (0, 0)),
-            pl.BlockSpec((slot_count, held_rows, tile), lambda j: (0, 0, j)),
-        ]
-        + [pl.BlockSpec(memory_space=pl.ANY)] * len(after),
-        out_specs=pl.BlockSpec((units, tile), lambda j: (0, j)),
+        in_specs=[vmem] * 2 + [pl.BlockSpec(memory_space=pl.ANY)] * len(after),
+        out_specs=vmem,
         out_shape=jax.ShapeDtypeStruct((units, width), jnp.bfloat16),
+        compiler_params=pltpu.CompilerParams(vmem_limit_bytes=VMEM_BYTES),
         cost_estimate=cost(2 * units * held * width),
     )(leave, rows, *after)
 
 
 def near_kernel(chips, stay, rows, near, *rest):
     mine, *others = rest[-chips:]
-    flat = rows[...].reshape(-1, rows.shape[-1])
     shard = mine.shape[0]
-    total = jnp.dot(stay[...], flat, preferred_element_type=jnp.float32) + near[...].astype(jnp.float32)
-    mine[...] = total[:shard]
-    for d, other in enumerate(others):
-        other[...] = total[(d + 1) * shard : (d + 2) * shard].astype(jnp.bfloat16)
+
+    def some(at):
+        flat = rows[:, :, at].reshape(stay.shape[1], -1)
+        total = jnp.dot(stay[...], flat, preferred_element_type=jnp.float32) + near[:, at].astype(jnp.float32)
+        mine[:, at] = total[:shard]
+        for d, other in enumerate(others):
+            other[:, at] = total[(d + 1) * shard : (d + 2) * shard].astype(jnp.bfloat16)
+
+    columns(some, rows.shape[-1])
 
 
 def add_near(stay, rows, near, chips, after):
     units, held = stay.shape
     width = rows.shape[-1]
     shard = units // chips
-    tile = tile_of(width)
+    vmem = pl.BlockSpec(memory_space=pltpu.VMEM)
     return pl.pallas_call(
         functools.partial(near_kernel, chips),
-        grid=(width // tile,),
-        in_specs=[
-            pl.BlockSpec((units, held), lambda j: (0, 0)),
-            pl.BlockSpec(rows.shape[:2] + (tile,), lambda j: (0, 0, j)),
-            pl.BlockSpec((units, tile), lambda j: (0, j)),
-        ]
-        + [pl.BlockSpec(memory_space=pl.ANY)] * len(after),
-        out_specs=(pl.BlockSpec((shard, tile), lambda j: (0, j)),) * chips,
+        in_specs=[vmem] * 3 + [pl.BlockSpec(memory_space=pl.ANY)] * len(after),
+        out_specs=(vmem,) * chips,
         out_shape=(jax.ShapeDtypeStruct((shard, width), jnp.float32),)
         + (jax.ShapeDtypeStruct((shard, width), jnp.bfloat16),) * (chips - 1),
+        compiler_params=pltpu.CompilerParams(vmem_limit_bytes=VMEM_BYTES),
         cost_estimate=cost(2 * units * held * width),
     )(stay, rows, near, *after)
 
 
 def hold_kernel(*refs):
     pass
+
+
+def some_of(array):
+    return array[(slice(0, 1),) * (array.ndim - 2) + (slice(0, 16), slice(0, 128))]
 
 
 def hold(array, after):
@@ -285,15 +291,18 @@
         pairing = matching_index(replica_plan, first)
     group_sum, projected = [], jnp.zeros((slot_count * held_rows, hidden_units), jnp.float32)
     rows, far, others = None, [], []
-    early = ready[2:] + ([pairing.reshape(1)] if pairs else [])
+    early = [some_of(ready[2])] + ([pairing.reshape(1)] if pairs else [])
     for span, sent in zip(spans, ready):
         if rows is not None:
-            sent = hold(sent, [rows] + early)
-            early = others[:1] + [projected]
+            sent = hold(sent, [some_of(rows)] + early)
+            early = [some_of(others[0]), some_of(projected)]
         rows = lax.all_to_all(sent, "expert", split_axis=0, concat_axis=0, tiled=True)
-        away = other_core_part(leave, rows, others[:1])
+        after = [some_of(other) for other in others[:1]]
+        if span == spans[-1]:
+            after = after + [some_of(projected)]
+        away = other_core_part(leave, rows, after)
         near = lax.ppermute(away, "group", [(i, i ^ 1) for i in range(group_size)])
-        mine, *others = add_near(stay, rows, near, chips, far[:1])
+        mine, *others = add_near(stay, rows, near, chips, [some_of(other) for other in far[:1]])
         far = [
             lax.ppermute(other, "group", [(i, i ^ (2 * d + 2)) for i in range(group_size)])
             for d, other in enumerate(others)
@@ -308,7 +317,7 @@
 
     route_score = jnp.sum(projected * held_hidden.astype(jnp.float32), axis=1)
     returned = lax.all_to_all(
-        hold(route_score.reshape(slot_count, held_rows), others[:1]),
+        hold(route_score.reshape(slot_count, held_rows), [some_of(others[0])]),
         "expert",
         split_axis=0,
         concat_axis=0,

time: 213 us -> 251 us (1.18)
  the two profiles are of different devices: /device:TPU:0 before, /device:TPU:18 now
where the time goes in v1:
time: 251 us; the launch traced here: 247 us
  waiting for transfers between devices  119 us (47%)
  Pallas kernels  35.4 us (14%)
  starting transfers between devices  33.6 us (13%)
  local copies, waits for them, and re-layouts  27.8 us (11%)
  other arithmetic  15.5 us (6%)
  matrix products  13 us (5%)
    all_to_all x3, waiting for transfers between devices, local(): lax.all_to_all(sent, 'expert', split_axis=0, concat_axis=0, tiled=True)  49.8 us
    ppermute x1, waiting for transfers between devices, local(): lax.switch(pairing, [functools.partial(lax.ppermute, axis_name='expert',...  41 us
    ppermute x3, waiting for transfers between devices, local(): lax.ppermute(other, 'group', [(i, i ^ 2 * d + 2) for i in range(group_siz...  25.5 us
    all_to_all x3, starting transfers between devices, local(): lax.all_to_all(sent, 'expert', split_axis=0, concat_axis=0, tiled=True)  20.7 us
    pallas_call x3, Pallas kernels, all_rows_to_send(): pl.pallas_call(send_all_kernel, grid=((stop - start) // tile,), in_specs=...  14.3 us
    dot_general x3, matrix products, local(): lax.dot_general(rows.reshape(slot_count * held_rows, -1), down_weight[0,...  13 us
    unnamed x32, local copies, waits for them, and re-layouts  12 us
    pallas_call x3, Pallas kernels, add_near(): pl.pallas_call(functools.partial(near_kernel, chips), in_specs=[vmem] * 3...  9.71 us
  transfers between devices with their start and end apart: 11, of which 6 were waited for; matrix products, arithmetic and copies ran while one was open for 18% of the time, Pallas kernels for 7%

profile of v1, /device:TPU:18, one launch (start us, length us, event | category | flops | bytes accessed | tf_op | source)
XLA Modules:
  0.0 246.7 jit_solution(636716084372594054)
XLA Ops:
  0.6 1.9 shard_map.103
  2.6 4.5 %shard_map.104 = bf16[8,80,2048]{2,1,0:T(8,128)(2,1)} custom-call(s32[1]{0:T(128)} %bitcast.seat, bf16[8,80,256]{2,1,0:T(8,128)(2,1)} %get-tuple-element.439.spread, bf16[256,3584]{1,0:T(8,128)(2,1)} %rows.5), custom_call_target="tpu_custom_call" | custom-call | flops 671088640 | bytes 2236962 | tf_op jit(solution)/shard_map/pallas_call | solution.py:106
  7.1 6.2 %all-to-all-start = ((bf16[8,80,2048]{2,1,0:T(8,128)(2,1)}), bf16[8,80,2048]{2,1,0:T(8,128)(2,1)S(1)}, u32[]{:S(2)}, u32[]{:S(2)}) async-start(bf16[8,80,2048]{2,1,0:T(8,128)(2,1)} %shard_map.104), calls=%async_computation | async-start | bytes 5242880 | tf_op jit(solution)/shard_map/all_to_all | solution.py:299
  13.2 4.4 %reshape.47 = bf16[2,2,256,640]{2,1,0,3:T(2,128)(2,1)} reshape(bf16[1024,640]{0,1:T(8,128)(2,1)} %bitcast.49) | data formatting | bytes 2621440 | tf_op jit(solution)/shard_map/reshape | solution.py:280
  17.6 3.0 %constant_dynamic-slice_fusion = (bf16[1,2,256,640]{2,1,0,3:T(2,128)(2,1)S(1)}, bf16[1,2,256,640]{2,1,0,3:T(2,128)(2,1)}) fusion(bf16[2,2,256,640]{2,1,0,3:T(2,128)(2,1)} %reshape.47, s32[]{:T(128)S(6)} %select_n.47, s32[]{:T(128)S(6)} %select_n.46), kind=kLoop, calls=%fused_computation.28 | loop fusion | bytes 2621448 | tf_op jit(solution)/shard_map/dynamic_slice | solution.py:281
  20.6 2.9 %copy.22 = bf16[1,2,256,640]{3,2,0,1:T(8,128)(2,1)} copy(bf16[1,2,256,640]{2,1,0,3:T(2,128)(2,1)} %get-tuple-element.455) | data formatting | bytes 1310720
  23.6 1.9 copy.23
  25.5 4.3 %shard_map.106.refs_0_ = bf16[8,80,640]{2,1,0:T(8,128)(2,1)} custom-call(s32[1]{0:T(128)} %bitcast.seat, bf16[8,80,256]{2,1,0:T(8,128)(2,1)} %get-tuple-element.439.spread, bf16[256,3584]{1,0:T(8,128)(2,1)} %rows.5), custom_call_target="tpu_custom_call" | custom-call | flops 209715200 | bytes 699050 | tf_op jit(solution)/shard_map/pallas_call | solution.py:106
  29.8 1.3 slice.54.refs_2_
  31.0 0.2 convert_reduce_fusion
  31.2 0.6 select_reduce_fusion
  31.8 1.1 fusion.15
  33.0 1.2 fusion.16
  34.2 1.9 fusion.17
  36.0 2.3 fusion.12
  38.3 31.1 %all-to-all-done.rows = bf16[8,80,2048]{2,1,0:T(8,128)(2,1)S(1)} async-done(((bf16[8,80,2048]{2,1,0:T(8,128)(2,1)}), bf16[8,80,2048]{2,1,0:T(8,128)(2,1)S(1)}, u32[]{:S(2)}, u32[]{:S(2)}) %all-to-all-start) | async-done | bytes 2621472 | tf_op jit(solution)/shard_map/all_to_all | solution.py:299
  69.4 1.1 copy-done
  70.5 3.6 %shard_map.108 = bf16[512,2048]{1,0:T(8,128)(2,1)} custom-call(bf16[512,640]{1,0:T(8,128)(2,1)S(1)} %bitcast.46, bf16[8,80,2048]{2,1,0:T(8,128)(2,1)S(1)} %all-to-all-done.rows), custom_call_target="tpu_custom_call" | custom-call | flops 1342177280 | bytes 4473924 | tf_op jit(solution)/shard_map/pallas_call | solution.py:141
  74.2 1.2 fusion.14
  76.7 5.5 %shard_map.105.refs_0_ = bf16[8,80,896]{2,1,0:T(8,128)(2,1)} custom-call(s32[1]{0:T(128)} %bitcast.seat, bf16[8,80,256]{2,1,0:T(8,128)(2,1)} %get-tuple-element.439.spread, bf16[256,3584]{1,0:T(8,128)(2,1)} %rows.5), custom_call_target="tpu_custom_call" | custom-call | flops 293601280 | bytes 978670 | tf_op jit(solution)/shard_map/pallas_call | solution.py:106
  82.2 0.6 slice.53.refs_1_
  82.8 7.4 %all-to-all-start.1 = ((bf16[8,80,896]{2,1,0:T(8,128)(2,1)}), bf16[8,80,896]{2,1,0:T(8,128)(2,1)}, u32[]{:S(2)}, u32[]{:S(2)}) async-start(bf16[8,80,896]{2,1,0:T(8,128)(2,1)} %shard_map.107), calls=%async_computation.1 | async-start | bytes 2293760 | tf_op jit(solution)/shard_map/all_to_all | solution.py:299
  90.2 4.7 %fusion = f32[640,1024]{1,0:T(8,128)S(1)} fusion(bf16[640,2048]{1,0:T(8,128)(2,1)S(1)} %bitcast.41, bf16[1,1024,3584]{2,1,0:T(8,128)(2,1)} %param.223), kind=kOutput, calls=%fused_computation | convolution fusion | flops 2684354560 | bytes 9437184 | tf_op jit(solution)/shard_map/dot_general | solution.py:311
  95.0 1.5 copy-done.13
  96.5 0.6 slice.56.refs_3_
  97.1 18.7 %all-to-all-done.1.rows = bf16[8,80,896]{2,1,0:T(8,128)(2,1)} async-done(((bf16[8,80,896]{2,1,0:T(8,128)(2,1)}), bf16[8,80,896]{2,1,0:T(8,128)(2,1)}, u32[]{:S(2)}, u32[]{:S(2)}) %all-to-all-start.1) | async-done | bytes 1146912 | tf_op jit(solution)/shard_map/all_to_all | solution.py:299
  115.8 1.3 slice.55.refs_1_
  117.1 0.0 collective-permute-done.210.near
  117.1 4.9 %shard_map.109 = (f32[256,2048]{1,0:T(8,128)S(1)}, bf16[256,2048]{1,0:T(8,128)(2,1)}) custom-call(bf16[512,640]{1,0:T(8,128)(2,1)S(1)} %bitcast.43, bf16[8,80,2048]{2,1,0:T(8,128)(2,1)S(1)} %all-to-all-done.rows, bf16[512,2048]{1,0:T(8,128)(2,1)} %collective-permute-done.210.near), custom_call_target="tpu_custom_call" | custom-call | flops 1342177280 | bytes 4473924 | tf_op jit(solution)/shard_map/pallas_call | solution.py:170
  122.0 1.3 copy-done.2
  123.3 1.3 slice.45.refs_2_.rest_0_
  124.6 7.1 %all-to-all-start.2 = ((bf16[8,80,640]{2,1,0:T(8,128)(2,1)}), bf16[8,80,640]{2,1,0:T(8,128)(2,1)S(1)}, u32[]{:S(2)}, u32[]{:S(2)}) async-start(bf16[8,80,640]{2,1,0:T(8,128)(2,1)} %shard_map.110), calls=%async_computation.2 | async-start | bytes 1638400 | tf_op jit(solution)/shard_map/all_to_all | solution.py:299
  131.8 0.5 collective-permute-start.212
  132.3 2.4 shard_map.111
  134.8 0.1 collective-permute-start.211
  134.8 3.4 %fusion.7 = f32[640,1024]{1,0:T(8,128)S(1)} fusion(f32[640,1024]{1,0:T(8,128)S(1)} %copy-done.14, bf16[640,896]{1,0:T(8,128)(2,1)} %bitcast.8, bf16[1,1024,3584]{2,1,0:T(8,128)(2,1)} %param.223), kind=kOutput, calls=%fused_computation.12 | convolution fusion | flops 1175060480 | bytes 8224768 | tf_op jit(solution)/shard_map/dot_general | solution.py:311
  138.3 18.3 %collective-permute-done.212 = bf16[256,2048]{1,0:T(8,128)(2,1)S(1)} collective-permute-done((bf16[256,2048]{1,0:T(8,128)(2,1)}, bf16[256,2048]{1,0:T(8,128)(2,1)S(1)}, u32[]{:S(2)}, u32[]{:S(2)}) %collective-permute-start.212) | collective-permute-done | bytes 1048608 | tf_op jit(solution)/shard_map/ppermute | solution.py:307
  156.6 0.0 collective-permute-done.211.near
  156.6 3.3 %shard_map.112 = (f32[256,896]{1,0:T(8,128)S(1)}, bf16[256,896]{1,0:T(8,128)(2,1)}) custom-call(bf16[512,640]{1,0:T(8,128)(2,1)S(1)} %bitcast.44, bf16[8,80,896]{2,1,0:T(8,128)(2,1)} %all-to-all-done.1.rows, bf16[512,896]{1,0:T(8,128)(2,1)S(1)} %collective-permute-done.211.near, bf16[16,128]{1,0:T(8,128)(2,1)S(1)} %slice.57.rest_0_), custom_call_target="tpu_custom_call" | custom-call | flops 587202560 | bytes 1957341 | tf_op jit(solution)/shard_map/pallas_call | solution.py:170
  159.9 0.7 slice.49.rest_0_
  160.6 1.6 shard_map.113
  162.3 0.5 collective-permute-start.214
  162.8 4.9 %fusion.18 = (bf16[640,1024]{1,0:T(8,128)(2,1)}, f32[640]{0:T(1024)S(1)}) fusion(bf16[1,1,8,80,1024]{4,3,2,1,0:T(8,128)(2,1)} %param.224, f32[640,1024]{1,0:T(8,128)} %copy-done.7, bf16[640,640]{1,0:T(8,128)(2,1)S(1)} %bitcast.42, bf16[1,1024,3584]{2,1,0:T(8,128)(2,1)} %param.223), kind=kOutput, calls=%fused_computation.37 | convolution fusion | flops 842136960 | bytes 7375360 | tf_op jit(solution)/shard_map/dot_general | solution.py:311
  167.6 0.7 reshape.49.refs_0_
  168.3 7.2 %collective-permute-done.214 = bf16[256,896]{1,0:T(8,128)(2,1)} collective-permute-done((bf16[256,896]{1,0:T(8,128)(2,1)}, bf16[256,896]{1,0:T(8,128)(2,1)}, u32[]{:S(2)}, u32[]{:S(2)}) %collective-permute-start.214) | collective-permute-done | bytes 458784 | tf_op jit(solution)/shard_map/ppermute | solution.py:307
  175.5 0.7 slice.59.rest_0_
  176.2 0.8 copy-done.4
  177.0 1.1 copy-done.5
  178.1 1.5 shard_map.114
  179.6 0.5 collective-permute-start.215
  180.1 1.3 slice.52.refs_1_
  181.4 1.5 add_convert_fusion.1
  183.0 6.0 %all-to-all-start.3 = ((f32[8,1,80]{2,1,0:T(1,128)}), f32[8,1,80]{2,1,0:T(1,128)S(1)}, u32[]{:S(2)}, u32[]{:S(2)}) async-start(f32[8,1,80]{2,1,0:T(1,128)} %bitcast.51), calls=%async_computation.3 | async-start | bytes 8192 | tf_op jit(solution)/shard_map/all_to_all | solution.py:319
  189.0 1.1 add_convert_fusion.2
  190.1 2.9 %all-to-all-done.3 = f32[8,1,80]{2,1,0:T(1,128)S(1)} async-done(((f32[8,1,80]{2,1,0:T(1,128)}), f32[8,1,80]{2,1,0:T(1,128)S(1)}, u32[]{:S(2)}, u32[]{:S(2)}) %all-to-all-start.3) | async-done | bytes 2592 | tf_op jit(solution)/shard_map/all_to_all | solution.py:319
  193.0 0.6 copy-done.10
  193.6 1.8 shard_map.116
  195.4 0.7 copy-done.9
  196.1 1.0 add_convert_fusion.3
  197.2 0.1 pad_maximum_fusion
  197.3 46.2 %conditional.4 = (bf16[256,3584]{1,0:T(8,128)(2,1)}) conditional(s32[]{:T(128)} %clamp.3, bf16[256,3584]{1,0:T(8,128)(2,1)S(1)} %pad_maximum_fusion, bf16[256,3584]{1,0:T(8,128)(2,1)S(1)} %pad_maximum_fusion, bf16[256,3584]{1,0:T(8,128)(2,1)S(1)} %pad_maximum_fusion, ...), branch_computations={%region_8.9_spmd, %region_9.10_spmd, %region_10.11_spmd, %region_1... | conditional | bytes 7340080
  197.4 5.2 %collective-permute-start.99 = (bf16[256,3584]{1,0:T(8,128)(2,1)S(1)}, bf16[256,3584]{1,0:T(8,128)(2,1)}, u32[]{:S(2)}, u32[]{:S(2)}) collective-permute-start(bf16[256,3584]{1,0:T(8,128)(2,1)S(1)} %param.99), channel_id=1, source_target_pairs={{0,4},{6,7},{4,0},{7,6},{8,12},{14,15},{12,8},{15,14},{16,20},{22,... | collective-permute-start | bytes 5505032 | tf_op jit(solution)/shard_map/cond/branch_99_fun/ppermute | solution.py:333
  202.5 41.0 %collective-permute-done.99 = bf16[256,3584]{1,0:T(8,128)(2,1)} collective-permute-done((bf16[256,3584]{1,0:T(8,128)(2,1)S(1)}, bf16[256,3584]{1,0:T(8,128)(2,1)}, u32[]{:S(2)}, u32[]{:S(2)}) %collective-permute-start.99) | collective-permute-done | bytes 1835040 | tf_op jit(solution)/shard_map/cond/branch_99_fun/ppermute | solution.py:333
  243.5 3.2 %fusion.3 = bf16[1,256,3584]{2,1,0:T(8,128)(2,1)} fusion(bf16[256,3584]{1,0:T(8,128)(2,1)} %get-tuple-element.456, bf16[256,640]{1,0:T(8,128)(2,1)S(1)} %add_convert_fusion.3, bf16[256,896]{1,0:T(8,128)(2,1)S(1)} %add_convert_fusion.2, bf16[256,2048]{1,0:T(8,128)(2,1)S(1)} %add_convert_fusion.1), kind=kLoop, calls=%fused_computation.6 | loop fusion | flops 8257536 | bytes 5505024 | tf_op jit(solution)/shard_map/reshape | solution.py:341
  (33 shorter events, 0.1 us)
Async XLA Ops:
  7.1 62.4 %all-to-all-start = ((bf16[8,80,2048]{2,1,0:T(8,128)(2,1)}), bf16[8,80,2048]{2,1,0:T(8,128)(2,1)S(1)}, u32[]{:S(2)}, u32[]{:S(2)}) async-start(bf16[8,80,2048]{2,1,0:T(8,128)(2,1)} %shard_map.104), calls=%async_computation | async-start | bytes 5242880 | tf_op jit(solution)/shard_map/all_to_all | solution.py:299
  23.6 7.5 %copy-start.11 = (s32[8]{0:T(128)S(1)}, s32[8]{0:T(128)}, u32[]{:S(2)}) copy-start(s32[8]{0:T(128)} %slot_plan.1) | copy-start | bytes 100
  69.4 1.1 copy-start
  70.5 3.6 %copy-start.12 = (s32[256]{0:T(256)S(1)}, s32[256]{0:T(256)}, u32[]{:S(2)}) copy-start(s32[256]{0:T(256)} %constant.49.clone) | copy-start | bytes 3076
  74.2 42.9 %collective-permute-start.210 = (bf16[512,2048]{1,0:T(8,128)(2,1)}, bf16[512,2048]{1,0:T(8,128)(2,1)}, u32[]{:S(2)}, u32[]{:S(2)}) collective-permute-start(bf16[512,2048]{1,0:T(8,128)(2,1)} %shard_map.108), channel_id=1, source_target_pairs={{0,8},{8,0},{16,24},{24,16},{1,9},{9,1},{17,25},{25,17},{2,10},{10... | collective-permute-start | bytes 6291464 | tf_op jit(solution)/shard_map/ppermute | solution.py:304
  82.8 33.0 %all-to-all-start.1 = ((bf16[8,80,896]{2,1,0:T(8,128)(2,1)}), bf16[8,80,896]{2,1,0:T(8,128)(2,1)}, u32[]{:S(2)}, u32[]{:S(2)}) async-start(bf16[8,80,896]{2,1,0:T(8,128)(2,1)} %shard_map.107), calls=%async_computation.1 | async-start | bytes 2293760 | tf_op jit(solution)/shard_map/all_to_all | solution.py:299
  95.0 1.5 copy-start.13
  122.0 1.3 copy-start.2
  123.3 9.0 %copy-start.1 = (bf16[2,1,256,640]{3,2,0,1:T(8,128)(2,1)S(1)}, bf16[2,1,256,640]{3,2,0,1:T(8,128)(2,1)}, u32[]{:S(2)}) copy-start(bf16[2,1,256,640]{3,2,0,1:T(8,128)(2,1)} %get-tuple-element.452) | copy-start | bytes 1966084
  124.6 7.7 %copy-start.6 = (bf16[16,128]{1,0:T(8,128)(2,1)S(1)}, bf16[16,128]{1,0:T(8,128)(2,1)}, u32[]{:S(2)}) copy-start(bf16[16,128]{1,0:T(8,128)(2,1)} %slice.45.refs_2_.rest_0_) | copy-start | bytes 12292
  124.6 36.0 %all-to-all-start.2 = ((bf16[8,80,640]{2,1,0:T(8,128)(2,1)}), bf16[8,80,640]{2,1,0:T(8,128)(2,1)S(1)}, u32[]{:S(2)}, u32[]{:S(2)}) async-start(bf16[8,80,640]{2,1,0:T(8,128)(2,1)} %shard_map.110), calls=%async_computation.2 | async-start | bytes 1638400 | tf_op jit(solution)/shard_map/all_to_all | solution.py:299
  131.8 3.1 %copy-start.14 = (f32[640,1024]{1,0:T(8,128)S(1)}, f32[640,1024]{1,0:T(8,128)}, u32[]{:S(2)}) copy-start(f32[640,1024]{1,0:T(8,128)} %copy-done.13) | copy-start | bytes 7864324
  131.8 24.8 %collective-permute-start.212 = (bf16[256,2048]{1,0:T(8,128)(2,1)}, bf16[256,2048]{1,0:T(8,128)(2,1)S(1)}, u32[]{:S(2)}, u32[]{:S(2)}) collective-permute-start(bf16[256,2048]{1,0:T(8,128)(2,1)} %get-tuple-element.440), channel_id=1, source_target_pairs={{0,16},{8,24},{16,0},{24,8},{1,17},{9,25},{17,1},{25,9},{2,18},{10... | collective-permute-start | bytes 3145736 | tf_op jit(solution)/shard_map/ppermute | solution.py:307
  134.8 21.8 %collective-permute-start.211 = (bf16[512,896]{1,0:T(8,128)(2,1)S(1)}, bf16[512,896]{1,0:T(8,128)(2,1)S(1)}, u32[]{:S(2)}, u32[]{:S(2)}) collective-permute-start(bf16[512,896]{1,0:T(8,128)(2,1)S(1)} %shard_map.111), channel_id=1, source_target_pairs={{0,8},{8,0},{16,24},{24,16},{1,9},{9,1},{17,25},{25,17},{2,10},{10... | collective-permute-start | bytes 2752520 | tf_op jit(solution)/shard_map/ppermute | solution.py:304
  138.3 18.3 %copy-start.7 = (f32[640,1024]{1,0:T(8,128)}, f32[640,1024]{1,0:T(8,128)S(1)}, u32[]{:S(2)}) copy-start(f32[640,1024]{1,0:T(8,128)S(1)} %fusion.7) | copy-start | bytes 7864324
  156.6 3.4 %copy-start.8 = (bf16[256,2048]{1,0:T(8,128)(2,1)}, bf16[256,2048]{1,0:T(8,128)(2,1)S(1)}, u32[]{:S(2)}) copy-start(bf16[256,2048]{1,0:T(8,128)(2,1)S(1)} %collective-permute-done.212) | copy-start | bytes 3145732
  162.3 13.9 %collective-permute-start.213 = (bf16[512,640]{1,0:T(8,128)(2,1)}, bf16[512,640]{1,0:T(8,128)(2,1)S(1)}, u32[]{:S(2)}, u32[]{:S(2)}) collective-permute-start(bf16[512,640]{1,0:T(8,128)(2,1)} %shard_map.113), channel_id=1, source_target_pairs={{0,8},{8,0},{16,24},{24,16},{1,9},{9,1},{17,25},{25,17},{2,10},{10... | collective-permute-start | bytes 1966088 | tf_op jit(solution)/shard_map/ppermute | solution.py:304
  162.3 13.2 %collective-permute-start.214 = (bf16[256,896]{1,0:T(8,128)(2,1)}, bf16[256,896]{1,0:T(8,128)(2,1)}, u32[]{:S(2)}, u32[]{:S(2)}) collective-permute-start(bf16[256,896]{1,0:T(8,128)(2,1)} %get-tuple-element.441), channel_id=1, source_target_pairs={{0,16},{8,24},{16,0},{24,8},{1,17},{9,25},{17,1},{25,9},{2,18},{10... | collective-permute-start | bytes 1376264 | tf_op jit(solution)/shard_map/ppermute | solution.py:307
  168.3 13.1 %copy-start.3 = (f32[256,2048]{1,0:T(8,128)S(1)}, f32[256,2048]{1,0:T(8,128)}, u32[]{:S(2)}) copy-start(f32[256,2048]{1,0:T(8,128)} %copy-done.2) | copy-start | bytes 6291460
  176.2 0.8 copy-start.4
  177.0 1.1 copy-start.5
  179.6 15.8 %collective-permute-start.215 = (bf16[256,640]{1,0:T(8,128)(2,1)}, bf16[256,640]{1,0:T(8,128)(2,1)S(1)}, u32[]{:S(2)}, u32[]{:S(2)}) collective-permute-start(bf16[256,640]{1,0:T(8,128)(2,1)} %get-tuple-element.442), channel_id=1, source_target_pairs={{0,16},{8,24},{16,0},{24,8},{1,17},{9,25},{17,1},{25,9},{2,18},{10... | collective-permute-start | bytes 983048 | tf_op jit(solution)/shard_map/ppermute | solution.py:307
  183.0 10.0 %all-to-all-start.3 = ((f32[8,1,80]{2,1,0:T(1,128)}), f32[8,1,80]{2,1,0:T(1,128)S(1)}, u32[]{:S(2)}, u32[]{:S(2)}) async-start(f32[8,1,80]{2,1,0:T(1,128)} %bitcast.51), calls=%async_computation.3 | async-start | bytes 8192 | tf_op jit(solution)/shard_map/all_to_all | solution.py:319
  193.0 0.6 copy-start.10
  195.4 0.7 copy-start.9
  197.4 46.1 %collective-permute-start.99 = (bf16[256,3584]{1,0:T(8,128)(2,1)S(1)}, bf16[256,3584]{1,0:T(8,128)(2,1)}, u32[]{:S(2)}, u32[]{:S(2)}) collective-permute-start(bf16[256,3584]{1,0:T(8,128)(2,1)S(1)} %param.99), channel_id=1, source_target_pairs={{0,4},{6,7},{4,0},{7,6},{8,12},{14,15},{12,8},{15,14},{16,20},{22,... | collective-permute-start | bytes 5505032 | tf_op jit(solution)/shard_map/cond/branch_99_fun/ppermute | solution.py:333
